TPU v7x, 512 devices: a whole 4x8x8 slice. The times are simulated.
512 devices in a mesh: space: 128 (over x, y, z_lo), vz: 4 (over z_hi, core).
Axes of the slice: x: 4, y: 8, z: 8 (z_hi: 2, z_lo: 4; z = z_hi * 4 + z_lo), core: 2. Of those that a mesh axis runs over, the one named last changes fastest.
Arguments:
- distribution: float32 [48, 256, 8, 2304], P('vz', 'space'), may hold values from 0 to 6, as said below
- collision_rate: float32 [256, 8], P('space'), may hold values from 0.5 to 2
Outputs:
- new_distribution: float32 [48, 256, 8, 2304], P('vz', 'space')
Inputs may be any that keep to these rules, and one draw needn't show every extreme that they name: `distribution`: every entry is positive.
All inputs are finite; a program needn't handle non-finite values.
Results may differ from a plain program's by a relative error of at most 0.000056.
Values sent between devices are 32-bit elements; how exact they have to be, the bound alone decides.
No kernel may reach another device: no remote copies, remote signals or barrier semaphores. Data moves between devices by JAX's collectives and lax.ppermute only.
A program may use at most 64 MiB of HBM per device.

v0:
```python
import jax
import jax.numpy as jnp
from jax import lax
from jax.sharding import PartitionSpec as P

V = 48
SWEEPS = 3
vel_max = 4.5
step_ratio = 0.1
collision_scale = 0.004
relax_scale = 0.5


def with_halo(block, sides, width, periodic):
    for axis, dim in sides:
        count = lax.axis_size(axis)
        forward = [(i, i + 1) for i in range(count - 1)]
        if periodic:
            forward.append((count - 1, 0))
        backward = [(target, source) for source, target in forward]
        low = lax.ppermute(
            lax.slice_in_dim(block, block.shape[dim] - width, None, axis=dim), axis, forward
        )
        high = lax.ppermute(lax.slice_in_dim(block, 0, width, axis=dim), axis, backward)
        block = jnp.concatenate([low, block, high], axis=dim)
    return block


def grid_speeds(position):
    return vel_max * (2.0 * position + 1.0 - V) / V


def velocity_columns():
    grid_values = grid_speeds(jnp.arange(V, dtype=jnp.float32))
    return (jnp.repeat(grid_values, V), jnp.tile(grid_values, V))


def beam_warming(middle, near_cells, far_cells, magnitude):
    return (
        middle
        - 0.5 * magnitude * (3.0 * middle - 4.0 * near_cells + far_cells)
        + 0.5 * magnitude * magnitude * (middle - 2.0 * near_cells + far_cells)
    )


def roll_transport(field_data, speed_cols, axis_id):
    positive = speed_cols > 0
    near_cells = jnp.where(
        positive, jnp.roll(field_data, 1, axis_id), jnp.roll(field_data, -1, axis_id)
    )
    far_cells = jnp.where(
        positive, jnp.roll(field_data, 2, axis_id), jnp.roll(field_data, -2, axis_id)
    )
    return beam_warming(field_data, near_cells, far_cells, step_ratio * jnp.abs(speed_cols))


def combine_planes(partial_value, vertical_speeds):
    zero_moment = partial_value[0]
    return jnp.stack(
        [
            jnp.sum(zero_moment, 0),
            jnp.sum(partial_value[1], 0),
            jnp.sum(partial_value[2], 0),
            jnp.sum(vertical_speeds * zero_moment, 0),
            jnp.sum(partial_value[3] + vertical_speeds * vertical_speeds * zero_moment, 0),
        ]
    )


def cell_state(moment_totals):
    grid_spacing = 2.0 * vel_max / V
    unnormalised_mass = moment_totals[0]
    drift_velocity_x = moment_totals[1] / unnormalised_mass
    drift_velocity_y = moment_totals[2] / unnormalised_mass
    drift_velocity_z = moment_totals[3] / unnormalised_mass
    thermal_energy = (
        moment_totals[4] / unnormalised_mass
        - drift_velocity_x * drift_velocity_x
        - drift_velocity_y * drift_velocity_y
        - drift_velocity_z * drift_velocity_z
    ) / 3.0
    return (
        unnormalised_mass * grid_spacing**3,
        drift_velocity_x,
        drift_velocity_y,
        drift_velocity_z,
        thermal_energy,
    )


def maxwellian(cell_entries, velocity_x_grid, velocity_y_grid, vertical_speeds):
    mass_density, drift_velocity_x, drift_velocity_y, drift_velocity_z, thermal_energy = (
        cell_entries
    )
    squared_spread = (
        (velocity_x_grid - drift_velocity_x) ** 2
        + (velocity_y_grid - drift_velocity_y) ** 2
        + (vertical_speeds - drift_velocity_z) ** 2
    )
    return (
        mass_density
        * (2.0 * jnp.pi * thermal_energy) ** (-1.5)
        * jnp.exp(-squared_spread / (2.0 * thermal_energy))
    )


def velocity_shifts(middle):
    zero_row = jnp.zeros(middle.shape[:-1] + (V,), middle.dtype)
    zero_one = jnp.zeros(middle.shape[:-1] + (1,), middle.dtype)
    upper_x_neighbour = jnp.concatenate([middle[..., V:], zero_row], axis=-1)
    lower_x_neighbour = jnp.concatenate([zero_row, middle[..., :-V]], axis=-1)
    upper_y_neighbour = jnp.concatenate([middle[..., 1:], zero_one], axis=-1)
    lower_y_neighbour = jnp.concatenate([zero_one, middle[..., :-1]], axis=-1)
    return (upper_x_neighbour, lower_x_neighbour, upper_y_neighbour, lower_y_neighbour)


def relaxation_pass(
    bordered_grid,
    forcing_term,
    diagonal_factor,
    vertical_speeds,
    cell_entries,
    collide_rate,
    velocity_x_grid,
    velocity_y_grid,
    upper_mask,
    lower_mask,
):
    mass_density, drift_velocity_x, drift_velocity_y, drift_velocity_z, thermal_energy = (
        cell_entries
    )
    grid_spacing = 2.0 * vel_max / V
    stiffness_factor = thermal_energy / (grid_spacing * grid_spacing)
    half_timestep = 0.5 / grid_spacing
    middle = bordered_grid[1:-1]
    upper_x_neighbour, lower_x_neighbour, upper_y_neighbour, lower_y_neighbour = velocity_shifts(
        middle
    )
    running_total = forcing_term + collide_rate * (
        (stiffness_factor + (velocity_x_grid + grid_spacing - drift_velocity_x) * half_timestep)
        * upper_x_neighbour
        + (stiffness_factor - (velocity_x_grid - grid_spacing - drift_velocity_x) * half_timestep)
        * lower_x_neighbour
    )
    running_total = running_total + collide_rate * (
        (stiffness_factor + (velocity_y_grid + grid_spacing - drift_velocity_y) * half_timestep)
        * upper_mask
        * upper_y_neighbour
        + (stiffness_factor - (velocity_y_grid - grid_spacing - drift_velocity_y) * half_timestep)
        * lower_mask
        * lower_y_neighbour
    )
    running_total = running_total + collide_rate * (
        (stiffness_factor + (vertical_speeds + grid_spacing - drift_velocity_z) * half_timestep)
        * bordered_grid[2:]
        + (stiffness_factor - (vertical_speeds - grid_spacing - drift_velocity_z) * half_timestep)
        * bordered_grid[:-2]
    )
    return running_total / diagonal_factor


def shards(distribution, collision_rate):
    plane_count, column_count, row_count, velocity_width = distribution.shape
    half_width = velocity_width // 2
    velocity_x_grid, velocity_y_grid = velocity_columns()
    magnitude = step_ratio * jnp.abs(velocity_x_grid)
    extended = with_halo(distribution, (("space", 1),), 2, True)
    forward = beam_warming(
        distribution[..., half_width:],
        extended[:, 1 : column_count + 1, :, half_width:],
        extended[:, :column_count, :, half_width:],
        magnitude[half_width:],
    )
    backward = beam_warming(
        distribution[..., :half_width],
        extended[:, 3 : column_count + 3, :, :half_width],
        extended[:, 4 : column_count + 4, :, :half_width],
        magnitude[:half_width],
    )
    swept_x = jnp.concatenate([backward, forward], axis=-1)
    transported = roll_transport(swept_x, velocity_y_grid, 2)
    weights = jnp.stack(
        [
            jnp.ones_like(velocity_x_grid),
            velocity_x_grid,
            velocity_y_grid,
            velocity_x_grid * velocity_x_grid + velocity_y_grid * velocity_y_grid,
        ],
        axis=1,
    )
    partial_value = jnp.einsum(
        "zxyk,kw->wzxy", distribution, weights, precision=lax.Precision.HIGHEST
    )
    first_plane = lax.axis_index("vz") * plane_count
    local_speeds = grid_speeds(
        (first_plane + jnp.arange(plane_count, dtype=jnp.int32)).astype(jnp.float32)
    )
    moment_totals = lax.psum(combine_planes(partial_value, local_speeds[:, None, None]), "vz")
    cell_entries = tuple(
        (entry_array[None, :, :, None] for entry_array in cell_state(moment_totals))
    )
    grid_spacing = 2.0 * vel_max / V
    pointwise_rate = collision_rate[None, :, :, None]
    collide_rate = collision_scale * pointwise_rate
    relaxation_rate = relax_scale * pointwise_rate
    stiffness_factor = cell_entries[4] / (grid_spacing * grid_spacing)
    diagonal_factor = 1.0 + relaxation_rate + 6.0 * collide_rate * stiffness_factor
    index_y = jnp.arange(velocity_width, dtype=jnp.int32) % V
    upper_mask = (index_y < V - 1).astype(jnp.float32)
    lower_mask = (index_y > 0).astype(jnp.float32)
    vertical_speeds = local_speeds[:, None, None, None]
    forcing_term = transported + relaxation_rate * maxwellian(
        cell_entries, velocity_x_grid, velocity_y_grid, vertical_speeds
    )
    current_guess = transported
    for sweep_id in range(SWEEPS):
        bordered_grid = with_halo(current_guess, (("vz", 0),), 1, False)
        current_guess = relaxation_pass(
            bordered_grid,
            forcing_term,
            diagonal_factor,
            vertical_speeds,
            cell_entries,
            collide_rate,
            velocity_x_grid,
            velocity_y_grid,
            upper_mask,
            lower_mask,
        )
    return current_guess


def solution(mesh):
    return jax.shard_map(
        shards,
        mesh=mesh,
        in_specs=(P("vz", "space", None, None), P("space", None)),
        out_specs=P("vz", "space", None, None),
        check_vma=False,
    )
```

profile of v0, /device:TPU:1, one launch (start us, length us, event | category | flops | bytes accessed | tf_op | source)
XLA Modules:
  0.0 159.6 jit_solution(4560179693643808710)
XLA Ops:
  0.0 13.5 %collective-permute-start = (f32[12,2,8,2304]{3,2,1,0:T(8,128)}, f32[12,2,8,2304]{3,2,1,0:T(8,128)S(1)}, u32[]{:S(2)}, u32[]{:S(2)}) collective-permute-start(f32[12,2,8,2304]{3,2,1,0:T(8,128)} %param.2), channel_id=1, source_target_pairs={{4,0},{8,4},{12,8},{16,12},{20,16},{24,20},{28,24},{32,28},{36,32}... | collective-permute-start | bytes 5308424 | tf_op jit(solution)/shard_map/ppermute | solution.py:24
  13.5 1.9 %collective-permute-start.1 = (f32[12,2,8,2304]{3,2,1,0:T(8,128)}, f32[12,2,8,2304]{3,2,1,0:T(8,128)}, u32[]{:S(2)}, u32[]{:S(2)}) collective-permute-start(f32[12,2,8,2304]{3,2,1,0:T(8,128)} %param.2), channel_id=1, source_target_pairs={{0,4},{4,8},{8,12},{12,16},{16,20},{20,24},{24,28},{28,32},{32,36}... | collective-permute-start | bytes 5308424 | tf_op jit(solution)/shard_map/ppermute | solution.py:21
  15.5 0.6 broadcast_add_fusion.4
  16.1 0.6 add_multiply_fusion.1
  16.7 0.1 stack_tile.5
  16.8 0.1 broadcast_in_dim.25
  16.8 0.7 stack_reshape.5
  17.5 0.0 copy-done.1
  17.5 0.0 copy-done.2
  17.5 0.7 multiply_add_fusion.6
  18.3 0.0 copy-start
  18.3 10.0 %fusion = f32[4,12,2,8]{1,0,3,2:T(4,128)S(1)} fusion(f32[12,2,8,2304]{3,2,1,0:T(8,128)} %param.2, f32[2304,1]{0,1:T(1,128)S(1)} %multiply_add_fusion.6, f32[2304,1]{0,1:T(1,128)S(1)} %stack_tile.5, f32[2304,1]{0,1:T(1,128)} %stack_reshape.5, f32[4]{0:T(128)S(1)} %pad.24.clone), kind=kOutput, calls=%fused_computation.17 | convolution fusion | flops 21261312 | bytes 1800208 | tf_op jit(solution)/shard_map/zxyk,kw->wzxy/dot_general | solution.py:191
  28.2 0.8 slice_reduce_fusion
  29.0 0.7 reduce_sum.45
  29.7 1.2 constant_dynamic-update-slice_fusion.4
  30.9 1.3 constant_dynamic-update-slice_fusion.3
  32.2 1.3 constant_dynamic-update-slice_fusion.2
  33.4 0.8 add_reduce_fusion
  34.2 0.5 constant_dynamic-update-slice_fusion.1
  34.7 0.6 constant_dynamic-update-slice_fusion
  35.3 58.7 %psum.7 = f32[5,2,8]{2,1,0:T(2,128)S(1)} all-reduce(f32[5,2,8]{2,1,0:T(2,128)} %constant_dynamic-update-slice_fusion), channel_id=1, replica_groups=mesh['space'=128,'vz'=4] {'vz'}, use_global_device_ids=true, to_apply=%region_5.6 | all-reduce | flops 80 | bytes 640 | tf_op jit(solution)/shard_map/psum | solution.py:198
  94.0 0.6 bitcast_multiply_fusion
  94.6 1.3 broadcast_multiply_fusion.3
  95.9 0.6 copy-done.10
  96.5 1.4 multiply_add_fusion.7
  97.8 0.8 tile.38
  98.6 1.4 reshape.331
  100.1 1.4 copy.6
  101.4 1.4 copy.7
  102.8 1.4 copy.5
  104.2 0.7 broadcast_add_fusion.3
  105.0 0.9 multiply_add_fusion.4
  105.8 0.0 collective-permute-done
  105.9 0.0 collective-permute-done.1
  105.9 0.0 copy-done
  105.9 1.9 %multiply_add_fusion.2 = (f32[12,2,8,1152]{3,2,1,0:T(8,128)S(1)}, f32[12,2,8,1152]{3,2,1,0:T(8,128)S(1)}) fusion(f32[12,2,8,2304]{3,2,1,0:T(8,128)} %collective-permute-done.1, f32[12,2,8,2304]{3,2,1,0:T(8,128)S(1)} %copy-done, f32[1152]{0:T(1024)S(1)} %get-tuple-element.53, f32[1152]{0:T(1024)S(1)} %get-tuple-element.51, f32[1152]{0:T(1024)S(1)} %get-tuple-element.52, ...), kind=kLoop, calls=%fused_computation.53 | loop fusion | flops 5308416 | bytes 10649600 | tf_op jit(solution)/shard_map/add | solution.py:40
  107.8 0.3 fusion.26
  108.1 0.3 fusion.24
  108.4 0.4 fusion.4
  108.7 0.4 fusion.2
  109.1 2.0 %multiply_add_fusion.1 = f32[12,2,8,2304]{3,2,1,0:T(8,128)S(1)} fusion(f32[12,2,2,2304]{3,2,1,0:T(2,128)S(1)} %get-tuple-element.37, f32[12,2,6,2304]{3,2,1,0:T(8,128)S(1)} %get-tuple-element.39, f32[12,2,6,2304]{3,2,1,0:T(8,128)S(1)} %get-tuple-element.38, f32[12,2,2,2304]{3,2,1,0:T(2,128)S(1)} %get-tuple-element.36, ...), kind=kLoop, calls=%fused_computation.50 | loop fusion | flops 7962624 | bytes 10637568 | tf_op jit(solution)/shard_map/add | solution.py:40
  111.2 0.6 fusion.59
  111.8 2.1 %collective-permute-start.2 = (f32[1,2,8,2304]{3,2,1,0:T(8,128)S(1)}, f32[1,2,8,2304]{3,2,1,0:T(8,128)S(1)}, u32[]{:S(2)}, u32[]{:S(2)}) collective-permute-start(f32[1,2,8,2304]{3,2,1,0:T(8,128)S(1)} %get-tuple-element.30), channel_id=1, source_target_pairs={{1,0},{2,1},{3,2},{5,4},{6,5},{7,6},{9,8},{10,9},{11,10},{13,12},{... | collective-permute-start | bytes 442376 | tf_op jit(solution)/shard_map/ppermute | solution.py:24
  113.8 0.0 copy-start.4
  113.9 7.7 %collective-permute-start.3 = (f32[1,2,8,2304]{3,2,1,0:T(8,128)S(1)}, f32[1,2,8,2304]{3,2,1,0:T(8,128)S(1)}, u32[]{:S(2)}, u32[]{:S(2)}) collective-permute-start(f32[1,2,8,2304]{3,2,1,0:T(8,128)S(1)} %get-tuple-element.31), channel_id=1, source_target_pairs={{0,1},{1,2},{2,3},{4,5},{5,6},{6,7},{8,9},{9,10},{10,11},{12,13},{... | collective-permute-start | bytes 442376 | tf_op jit(solution)/shard_map/ppermute | solution.py:21
  121.6 0.6 fusion.58
  122.2 0.3 collective-permute-done.2
  122.5 1.4 collective-permute-done.3
  123.9 0.0 copy-done.5
  124.0 2.1 %fusion.22 = f32[12,2,8,2304]{3,2,1,0:T(8,128)S(1)} fusion(f32[12,2,8,2304]{3,2,1,0:T(8,128)S(1)} %multiply_add_fusion.1, f32[1,2,8,2304]{3,2,1,0:T(8,128)S(1)} %collective-permute-done.3, f32[1,2,8,2304]{3,2,1,0:T(8,128)S(1)} %collective-permute-done.2, f32[12,2,8,2303]{3,2,1,0:T(8,128)S(1)} %get-tuple-element.29, ...), kind=kLoop, calls=%fused_computation.44 | loop fusion | flops 10616832 | bytes 11576384 | tf_op jit(solution)/shard_map/div | solution.py:159
  126.1 0.6 fusion.56
  126.7 1.9 %collective-permute-start.4 = (f32[1,2,8,2304]{3,2,1,0:T(8,128)S(1)}, f32[1,2,8,2304]{3,2,1,0:T(8,128)S(1)}, u32[]{:S(2)}, u32[]{:S(2)}) collective-permute-start(f32[1,2,8,2304]{3,2,1,0:T(8,128)S(1)} %get-tuple-element.24), channel_id=1, source_target_pairs={{1,0},{2,1},{3,2},{5,4},{6,5},{7,6},{9,8},{10,9},{11,10},{13,12},{... | collective-permute-start | bytes 442376 | tf_op jit(solution)/shard_map/ppermute | solution.py:24
  128.6 8.6 %collective-permute-start.5 = (f32[1,2,8,2304]{3,2,1,0:T(8,128)S(1)}, f32[1,2,8,2304]{3,2,1,0:T(8,128)S(1)}, u32[]{:S(2)}, u32[]{:S(2)}) collective-permute-start(f32[1,2,8,2304]{3,2,1,0:T(8,128)S(1)} %get-tuple-element.25), channel_id=1, source_target_pairs={{0,1},{1,2},{2,3},{4,5},{5,6},{6,7},{8,9},{9,10},{10,11},{12,13},{... | collective-permute-start | bytes 442376 | tf_op jit(solution)/shard_map/ppermute | solution.py:21
  137.2 0.6 fusion.55
  137.8 0.2 collective-permute-done.4
  138.0 2.3 %collective-permute-done.5 = f32[1,2,8,2304]{3,2,1,0:T(8,128)S(1)} collective-permute-done((f32[1,2,8,2304]{3,2,1,0:T(8,128)S(1)}, f32[1,2,8,2304]{3,2,1,0:T(8,128)S(1)}, u32[]{:S(2)}, u32[]{:S(2)}) %collective-permute-start.5) | collective-permute-done | bytes 147488 | tf_op jit(solution)/shard_map/ppermute | solution.py:21
  140.3 2.0 %fusion.16 = f32[12,2,8,2304]{3,2,1,0:T(8,128)S(1)} fusion(f32[12,2,8,2304]{3,2,1,0:T(8,128)S(1)} %fusion.22, f32[1,2,8,2304]{3,2,1,0:T(8,128)S(1)} %collective-permute-done.5, f32[1,2,8,2304]{3,2,1,0:T(8,128)S(1)} %collective-permute-done.4, f32[12,2,8,2303]{3,2,1,0:T(8,128)S(1)} %get-tuple-element.23, f32[12,2,8,2303]{3,2,1,0:T(8,128)S(1)} %get-tuple-element.22, ...), kind=kLoop, calls=%fused_computation.36 | loop fusion | flops 10616832 | bytes 13345856 | tf_op jit(solution)/shard_map/div | solution.py:159
  142.4 0.6 fusion.53
  143.0 1.9 %collective-permute-start.6 = (f32[1,2,8,2304]{3,2,1,0:T(8,128)S(1)}, f32[1,2,8,2304]{3,2,1,0:T(8,128)S(1)}, u32[]{:S(2)}, u32[]{:S(2)}) collective-permute-start(f32[1,2,8,2304]{3,2,1,0:T(8,128)S(1)} %get-tuple-element.18), channel_id=1, source_target_pairs={{1,0},{2,1},{3,2},{5,4},{6,5},{7,6},{9,8},{10,9},{11,10},{13,12},{... | collective-permute-start | bytes 442376 | tf_op jit(solution)/shard_map/ppermute | solution.py:24
  145.0 8.4 %collective-permute-start.7 = (f32[1,2,8,2304]{3,2,1,0:T(8,128)S(1)}, f32[1,2,8,2304]{3,2,1,0:T(8,128)S(1)}, u32[]{:S(2)}, u32[]{:S(2)}) collective-permute-start(f32[1,2,8,2304]{3,2,1,0:T(8,128)S(1)} %get-tuple-element.19), channel_id=1, source_target_pairs={{0,1},{1,2},{2,3},{4,5},{5,6},{6,7},{8,9},{9,10},{10,11},{12,13},{... | collective-permute-start | bytes 442376 | tf_op jit(solution)/shard_map/ppermute | solution.py:21
  153.4 0.6 fusion.52
  154.0 0.4 collective-permute-done.6
  154.3 2.3 %collective-permute-done.7 = f32[1,2,8,2304]{3,2,1,0:T(8,128)S(1)} collective-permute-done((f32[1,2,8,2304]{3,2,1,0:T(8,128)S(1)}, f32[1,2,8,2304]{3,2,1,0:T(8,128)S(1)}, u32[]{:S(2)}, u32[]{:S(2)}) %collective-permute-start.7) | collective-permute-done | bytes 147488 | tf_op jit(solution)/shard_map/ppermute | solution.py:21
  156.7 2.9 %fusion.10 = f32[12,2,8,2304]{3,2,1,0:T(8,128)} fusion(f32[12,2,8,2304]{3,2,1,0:T(8,128)S(1)} %fusion.16, f32[1,2,8,2304]{3,2,1,0:T(8,128)S(1)} %collective-permute-done.7, f32[1,2,8,2304]{3,2,1,0:T(8,128)S(1)} %collective-permute-done.6, f32[12,2,8,2303]{3,2,1,0:T(8,128)S(1)} %get-tuple-element.17, f32[12,2,8,2303]{3,2,1,0:T(8,128)S(1)} %get-tuple-element.16, ...), kind=kLoop, calls=%fused_computation.28 | loop fusion | flops 10616832 | bytes 13345856 | tf_op jit(solution)/shard_map/div | solution.py:159
  (25 shorter events, 0.1 us)
Async XLA Ops:
  0.0 105.8 %collective-permute-start = (f32[12,2,8,2304]{3,2,1,0:T(8,128)}, f32[12,2,8,2304]{3,2,1,0:T(8,128)S(1)}, u32[]{:S(2)}, u32[]{:S(2)}) collective-permute-start(f32[12,2,8,2304]{3,2,1,0:T(8,128)} %param.2), channel_id=1, source_target_pairs={{4,0},{8,4},{12,8},{16,12},{20,16},{24,20},{28,24},{32,28},{36,32}... | collective-permute-start | bytes 5308424 | tf_op jit(solution)/shard_map/ppermute | solution.py:24
  13.5 92.3 %collective-permute-start.1 = (f32[12,2,8,2304]{3,2,1,0:T(8,128)}, f32[12,2,8,2304]{3,2,1,0:T(8,128)}, u32[]{:S(2)}, u32[]{:S(2)}) collective-permute-start(f32[12,2,8,2304]{3,2,1,0:T(8,128)} %param.2), channel_id=1, source_target_pairs={{0,4},{4,8},{8,12},{12,16},{16,20},{20,24},{24,28},{28,32},{32,36}... | collective-permute-start | bytes 5308424 | tf_op jit(solution)/shard_map/ppermute | solution.py:21
  16.7 0.9 copy-start.1
  16.8 0.7 copy-start.2
  18.3 87.6 %copy-start = (f32[12,2,8,2304]{3,2,1,0:T(8,128)S(1)}, f32[12,2,8,2304]{3,2,1,0:T(8,128)}, u32[]{:S(2)}) copy-start(f32[12,2,8,2304]{3,2,1,0:T(8,128)} %param.2) | copy-start | bytes 5308420
  95.9 0.6 copy-start.10
  111.8 10.8 %collective-permute-start.2 = (f32[1,2,8,2304]{3,2,1,0:T(8,128)S(1)}, f32[1,2,8,2304]{3,2,1,0:T(8,128)S(1)}, u32[]{:S(2)}, u32[]{:S(2)}) collective-permute-start(f32[1,2,8,2304]{3,2,1,0:T(8,128)S(1)} %get-tuple-element.30), channel_id=1, source_target_pairs={{1,0},{2,1},{3,2},{5,4},{6,5},{7,6},{9,8},{10,9},{11,10},{13,12},{... | collective-permute-start | bytes 442376 | tf_op jit(solution)/shard_map/ppermute | solution.py:24
  113.8 10.1 %copy-start.3 = (f32[12,2,8]{2,1,0:T(2,128)S(1)}, f32[12,2,8]{2,1,0:T(2,128)}, u32[]{:S(2)}) copy-start(f32[12,2,8]{2,1,0:T(2,128)} %copy.6) | copy-start | bytes 2308
  113.8 10.1 %copy-start.4 = (f32[12,2,8]{2,1,0:T(2,128)S(1)}, f32[12,2,8]{2,1,0:T(2,128)}, u32[]{:S(2)}) copy-start(f32[12,2,8]{2,1,0:T(2,128)} %copy.7) | copy-start | bytes 2308
  113.9 10.1 %copy-start.5 = (f32[12,2,8]{2,1,0:T(2,128)S(1)}, f32[12,2,8]{2,1,0:T(2,128)}, u32[]{:S(2)}) copy-start(f32[12,2,8]{2,1,0:T(2,128)} %copy.5) | copy-start | bytes 2308
  113.9 10.1 %copy-start.6 = (f32[2,8]{1,0:T(2,128)S(1)}, f32[2,8]{1,0:T(2,128)}, u32[]{:S(2)}) copy-start(f32[2,8]{1,0:T(2,128)} %get-tuple-element.61) | copy-start | bytes 196
  113.9 10.1 %copy-start.7 = (f32[2,8]{1,0:T(2,128)S(1)}, f32[2,8]{1,0:T(2,128)}, u32[]{:S(2)}) copy-start(f32[2,8]{1,0:T(2,128)} %get-tuple-element.62) | copy-start | bytes 196
  113.9 10.1 %copy-start.8 = (f32[2,8]{1,0:T(2,128)S(1)}, f32[2,8]{1,0:T(2,128)}, u32[]{:S(2)}) copy-start(f32[2,8]{1,0:T(2,128)} %get-tuple-element.63) | copy-start | bytes 196
  113.9 10.1 %copy-start.9 = (f32[2,8]{1,0:T(2,128)S(1)}, f32[2,8]{1,0:T(2,128)}, u32[]{:S(2)}) copy-start(f32[2,8]{1,0:T(2,128)} %get-tuple-element.65) | copy-start | bytes 196
  113.9 10.0 %collective-permute-start.3 = (f32[1,2,8,2304]{3,2,1,0:T(8,128)S(1)}, f32[1,2,8,2304]{3,2,1,0:T(8,128)S(1)}, u32[]{:S(2)}, u32[]{:S(2)}) collective-permute-start(f32[1,2,8,2304]{3,2,1,0:T(8,128)S(1)} %get-tuple-element.31), channel_id=1, source_target_pairs={{0,1},{1,2},{2,3},{4,5},{5,6},{6,7},{8,9},{9,10},{10,11},{12,13},{... | collective-permute-start | bytes 442376 | tf_op jit(solution)/shard_map/ppermute | solution.py:21
  126.7 11.3 %collective-permute-start.4 = (f32[1,2,8,2304]{3,2,1,0:T(8,128)S(1)}, f32[1,2,8,2304]{3,2,1,0:T(8,128)S(1)}, u32[]{:S(2)}, u32[]{:S(2)}) collective-permute-start(f32[1,2,8,2304]{3,2,1,0:T(8,128)S(1)} %get-tuple-element.24), channel_id=1, source_target_pairs={{1,0},{2,1},{3,2},{5,4},{6,5},{7,6},{9,8},{10,9},{11,10},{13,12},{... | collective-permute-start | bytes 442376 | tf_op jit(solution)/shard_map/ppermute | solution.py:24
  128.6 11.7 %collective-permute-start.5 = (f32[1,2,8,2304]{3,2,1,0:T(8,128)S(1)}, f32[1,2,8,2304]{3,2,1,0:T(8,128)S(1)}, u32[]{:S(2)}, u32[]{:S(2)}) collective-permute-start(f32[1,2,8,2304]{3,2,1,0:T(8,128)S(1)} %get-tuple-element.25), channel_id=1, source_target_pairs={{0,1},{1,2},{2,3},{4,5},{5,6},{6,7},{8,9},{9,10},{10,11},{12,13},{... | collective-permute-start | bytes 442376 | tf_op jit(solution)/shard_map/ppermute | solution.py:21
  143.0 11.3 %collective-permute-start.6 = (f32[1,2,8,2304]{3,2,1,0:T(8,128)S(1)}, f32[1,2,8,2304]{3,2,1,0:T(8,128)S(1)}, u32[]{:S(2)}, u32[]{:S(2)}) collective-permute-start(f32[1,2,8,2304]{3,2,1,0:T(8,128)S(1)} %get-tuple-element.18), channel_id=1, source_target_pairs={{1,0},{2,1},{3,2},{5,4},{6,5},{7,6},{9,8},{10,9},{11,10},{13,12},{... | collective-permute-start | bytes 442376 | tf_op jit(solution)/shard_map/ppermute | solution.py:24
  145.0 11.7 %collective-permute-start.7 = (f32[1,2,8,2304]{3,2,1,0:T(8,128)S(1)}, f32[1,2,8,2304]{3,2,1,0:T(8,128)S(1)}, u32[]{:S(2)}, u32[]{:S(2)}) collective-permute-start(f32[1,2,8,2304]{3,2,1,0:T(8,128)S(1)} %get-tuple-element.19), channel_id=1, source_target_pairs={{0,1},{1,2},{2,3},{4,5},{5,6},{6,7},{8,9},{9,10},{10,11},{12,13},{... | collective-permute-start | bytes 442376 | tf_op jit(solution)/shard_map/ppermute | solution.py:21
where the time goes:
time: 160 us
  blocking collectives  58.7 us (37%)
  starting transfers between devices  46 us (29%)
  other arithmetic  21.2 us (13%)
  local copies, waits for them, and re-layouts  16.4 us (10%)
  matrix products  9.96 us (6%)
  waiting for transfers between devices  6.96 us (4%)
    psum x1, blocking collectives, shards(): lax.psum(combine_planes(partial_value, local_speeds[:, None, None]), 'vz')  58.7 us
    ppermute x4, starting transfers between devices, with_halo(): lax.ppermute(lax.slice_in_dim(block, block.shape[dim] - width, None, axis...  26.6 us
    ppermute x4, starting transfers between devices, with_halo(): lax.ppermute(lax.slice_in_dim(block, 0, width, axis=dim), axis, backward)  19.4 us
    dot_general x1, matrix products, shards(): jnp.einsum('zxyk,kw->wzxy', distribution, weights, precision=lax.Precisio...  9.96 us
    div x3, other arithmetic, relaxation_pass(): return running_total / diagonal_factor  7.02 us
    ppermute x4, waiting for transfers between devices, with_halo(): lax.ppermute(lax.slice_in_dim(block, block.shape[dim] - width, None, axis...  6.09 us
    unnamed x26, local copies, waits for them, and re-layouts  4.9 us
    add x2, other arithmetic, beam_warming(): middle - 0.5 * magnitude * (3.0 * middle - 4.0 * near_cells + far_cells)  3.96 us
  transfers between devices with their start and end apart: 8, of which 6 were waited for; matrix products, arithmetic and copies ran while one was open for 21% of the time, Pallas kernels for 0%

commit v1 on v0

--- a/solution.py
+++ b/solution.py
@@ -195,7 +195,9 @@
     local_speeds = grid_speeds(
         (first_plane + jnp.arange(plane_count, dtype=jnp.int32)).astype(jnp.float32)
     )
-    moment_totals = lax.psum(combine_planes(partial_value, local_speeds[:, None, None]), "vz")
+    moment_totals = jnp.sum(
+        lax.all_gather(combine_planes(partial_value, local_speeds[:, None, None]), "vz"), axis=0
+    )
     cell_entries = tuple(
         (entry_array[None, :, :, None] for entry_array in cell_state(moment_totals))
     )

time: 160 us -> 162 us (1.012)
  blocking collectives: 58.7 us -> 62.7 us
  local copies, waits for them, and re-layouts: 16.4 us -> 13.5 us
    all_gather x0 -> x1, blocking collectives: none -> 62.7 us  [shards(): lax.all_gather(combine_planes(partial_value, local_speeds[:, None, None])...]
    psum x1 -> x0, blocking collectives: 58.7 us -> none  [shards(): lax.psum(combine_planes(partial_value, local_speeds[:, None, None]), 'vz')]
    unnamed x26 -> x28, local copies, waits for them, and re-layouts: 4.9 us -> 3.24 us
  transfers between devices with their start and end apart: 8 -> 8, of which waited for: 6 -> 6; matrix products, arithmetic and copies ran while one was open for 21% -> 18% of each run, Pallas kernels for 0% -> 0%
where the time goes in v1:
time: 162 us; the launch traced here: 161 us
  blocking collectives  62.7 us (39%)
  starting transfers between devices  45.8 us (28%)
  other arithmetic  21.2 us (13%)
  local copies, waits for them, and re-layouts  13.5 us (8%)
  matrix products  9.96 us (6%)
  waiting for transfers between devices  7.23 us (4%)
    all_gather x1, blocking collectives, shards(): lax.all_gather(combine_planes(partial_value, local_speeds[:, None, None])...  62.7 us
    ppermute x4, starting transfers between devices, with_halo(): lax.ppermute(lax.slice_in_dim(block, block.shape[dim] - width, None, axis...  26.3 us
    ppermute x4, starting transfers between devices, with_halo(): lax.ppermute(lax.slice_in_dim(block, 0, width, axis=dim), axis, backward)  19.5 us
    dot_general x1, matrix products, shards(): jnp.einsum('zxyk,kw->wzxy', distribution, weights, precision=lax.Precisio...  9.96 us
    div x3, other arithmetic, relaxation_pass(): return running_total / diagonal_factor  7.06 us
    ppermute x4, waiting for transfers between devices, with_halo(): lax.ppermute(lax.slice_in_dim(block, block.shape[dim] - width, None, axis...  6.36 us
    add x2, other arithmetic, beam_warming(): middle - 0.5 * magnitude * (3.0 * middle - 4.0 * near_cells + far_cells)  3.95 us
    unnamed x28, local copies, waits for them, and re-layouts  3.24 us
  transfers between devices with their start and end apart: 8, of which 6 were waited for; matrix products, arithmetic and copies ran while one was open for 18% of the time, Pallas kernels for 0%

profile of v1, /device:TPU:1, one launch (start us, length us, event | category | flops | bytes accessed | tf_op | source)
XLA Modules:
  0.0 160.8 jit_solution(8904349352850619390)
XLA Ops:
  0.0 13.5 %collective-permute-start = (f32[12,2,8,2304]{3,2,1,0:T(8,128)}, f32[12,2,8,2304]{3,2,1,0:T(8,128)S(1)}, u32[]{:S(2)}, u32[]{:S(2)}) collective-permute-start(f32[12,2,8,2304]{3,2,1,0:T(8,128)} %param.2), channel_id=1, source_target_pairs={{4,0},{8,4},{12,8},{16,12},{20,16},{24,20},{28,24},{32,28},{36,32}... | collective-permute-start | bytes 5308424 | tf_op jit(solution)/shard_map/ppermute | solution.py:24
  13.5 1.9 %collective-permute-start.1 = (f32[12,2,8,2304]{3,2,1,0:T(8,128)}, f32[12,2,8,2304]{3,2,1,0:T(8,128)}, u32[]{:S(2)}, u32[]{:S(2)}) collective-permute-start(f32[12,2,8,2304]{3,2,1,0:T(8,128)} %param.2), channel_id=1, source_target_pairs={{0,4},{4,8},{8,12},{12,16},{16,20},{20,24},{24,28},{28,32},{32,36}... | collective-permute-start | bytes 5308424 | tf_op jit(solution)/shard_map/ppermute | solution.py:21
  15.5 0.5 broadcast_add_fusion.5
  16.0 0.6 add_multiply_fusion.1
  16.6 0.1 stack_tile.5
  16.7 0.1 broadcast_in_dim.25
  16.8 0.1 stack_reshape.5
  16.9 0.0 copy-start.6
  16.9 0.3 copy-done.1
  17.2 0.2 copy-done.2
  17.4 0.1 copy-done.6
  17.5 0.0 copy-start
  17.5 10.0 %fusion = f32[4,12,2,8]{1,0,3,2:T(4,128)S(1)} fusion(f32[12,2,8,2304]{3,2,1,0:T(8,128)} %param.2, f32[2304,1]{0,1:T(1,128)S(1)} %multiply_add_fusion.6, f32[2304,1]{0,1:T(1,128)S(1)} %stack_tile.5, f32[2304,1]{0,1:T(1,128)} %copy-done.6, f32[4]{0:T(128)S(1)} %pad.24.clone), kind=kOutput, calls=%fused_computation.17 | convolution fusion | flops 21261312 | bytes 1800208 | tf_op jit(solution)/shard_map/zxyk,kw->wzxy/dot_general | solution.py:191
  27.5 0.8 slice_reduce_fusion
  28.2 0.7 reduce_sum.54
  28.9 0.7 constant_dynamic-update-slice_fusion.4
  29.6 0.7 constant_dynamic-update-slice_fusion.3
  30.3 0.7 constant_dynamic-update-slice_fusion.2
  31.0 0.8 add_reduce_fusion
  31.7 62.7 %all-gather = f32[20,2,8]{2,1,0:T(2,128)} all-gather(f32[5,2,8]{2,1,0:T(2,128)S(1)} %constant_dynamic-update-slice_fusion), channel_id=2, replica_groups=mesh['space'=128,'vz'=4] {'vz'}, dimensions={0}, use_global_device_ids=true | all-gather | bytes 1600 | tf_op jit(solution)/shard_map/all_gather | solution.py:199
  94.4 0.7 reduce_sum.59
  95.2 0.6 bitcast_multiply_fusion
  95.8 1.3 broadcast_multiply_fusion.3
  97.1 0.6 copy-done.11
  97.6 1.4 multiply_add_fusion.7
  99.0 0.8 tile.38
  99.8 1.4 reshape.331
  101.2 1.4 copy.11
  102.6 1.4 copy.12
  104.0 1.4 copy.10
  105.4 0.7 broadcast_add_fusion.3
  106.1 0.9 multiply_add_fusion.4
  107.0 0.0 collective-permute-done
  107.0 0.0 collective-permute-done.1
  107.0 0.0 copy-done
  107.0 1.9 %multiply_add_fusion.2 = (f32[12,2,8,1152]{3,2,1,0:T(8,128)S(1)}, f32[12,2,8,1152]{3,2,1,0:T(8,128)S(1)}) fusion(f32[12,2,8,2304]{3,2,1,0:T(8,128)} %collective-permute-done.1, f32[12,2,8,2304]{3,2,1,0:T(8,128)S(1)} %copy-done, f32[1152]{0:T(1024)S(1)} %get-tuple-element.53, f32[1152]{0:T(1024)S(1)} %get-tuple-element.51, f32[1152]{0:T(1024)S(1)} %get-tuple-element.52, ...), kind=kLoop, calls=%fused_computation.53 | loop fusion | flops 5308416 | bytes 10649600 | tf_op jit(solution)/shard_map/add | solution.py:40
  109.0 0.3 fusion.26
  109.3 0.3 fusion.24
  109.5 0.4 fusion.4
  109.9 0.4 fusion.2
  110.3 2.0 %multiply_add_fusion.1 = f32[12,2,8,2304]{3,2,1,0:T(8,128)S(1)} fusion(f32[12,2,2,2304]{3,2,1,0:T(2,128)S(1)} %get-tuple-element.37, f32[12,2,6,2304]{3,2,1,0:T(8,128)S(1)} %get-tuple-element.39, f32[12,2,6,2304]{3,2,1,0:T(8,128)S(1)} %get-tuple-element.38, f32[12,2,2,2304]{3,2,1,0:T(2,128)S(1)} %get-tuple-element.36, ...), kind=kLoop, calls=%fused_computation.50 | loop fusion | flops 7962624 | bytes 10637568 | tf_op jit(solution)/shard_map/add | solution.py:40
  112.3 0.6 fusion.59
  112.9 2.1 %collective-permute-start.2 = (f32[1,2,8,2304]{3,2,1,0:T(8,128)S(1)}, f32[1,2,8,2304]{3,2,1,0:T(8,128)S(1)}, u32[]{:S(2)}, u32[]{:S(2)}) collective-permute-start(f32[1,2,8,2304]{3,2,1,0:T(8,128)S(1)} %get-tuple-element.30), channel_id=1, source_target_pairs={{1,0},{2,1},{3,2},{5,4},{6,5},{7,6},{9,8},{10,9},{11,10},{13,12},{... | collective-permute-start | bytes 442376 | tf_op jit(solution)/shard_map/ppermute | solution.py:24
  115.0 0.0 copy-start.4
  115.1 7.5 %collective-permute-start.3 = (f32[1,2,8,2304]{3,2,1,0:T(8,128)S(1)}, f32[1,2,8,2304]{3,2,1,0:T(8,128)S(1)}, u32[]{:S(2)}, u32[]{:S(2)}) collective-permute-start(f32[1,2,8,2304]{3,2,1,0:T(8,128)S(1)} %get-tuple-element.31), channel_id=1, source_target_pairs={{0,1},{1,2},{2,3},{4,5},{5,6},{6,7},{8,9},{9,10},{10,11},{12,13},{... | collective-permute-start | bytes 442376 | tf_op jit(solution)/shard_map/ppermute | solution.py:21
  122.6 0.6 fusion.58
  123.3 0.1 collective-permute-done.2
  123.4 1.7 %collective-permute-done.3 = f32[1,2,8,2304]{3,2,1,0:T(8,128)S(1)} collective-permute-done((f32[1,2,8,2304]{3,2,1,0:T(8,128)S(1)}, f32[1,2,8,2304]{3,2,1,0:T(8,128)S(1)}, u32[]{:S(2)}, u32[]{:S(2)}) %collective-permute-start.3) | collective-permute-done | bytes 147488 | tf_op jit(solution)/shard_map/ppermute | solution.py:21
  125.1 0.0 copy-done.4
  125.1 2.1 %fusion.22 = f32[12,2,8,2304]{3,2,1,0:T(8,128)S(1)} fusion(f32[12,2,8,2304]{3,2,1,0:T(8,128)S(1)} %multiply_add_fusion.1, f32[1,2,8,2304]{3,2,1,0:T(8,128)S(1)} %collective-permute-done.3, f32[1,2,8,2304]{3,2,1,0:T(8,128)S(1)} %collective-permute-done.2, f32[12,2,8,2303]{3,2,1,0:T(8,128)S(1)} %get-tuple-element.29, ...), kind=kLoop, calls=%fused_computation.44 | loop fusion | flops 10616832 | bytes 11576384 | tf_op jit(solution)/shard_map/div | solution.py:159
  127.2 0.6 fusion.56
  127.8 1.9 %collective-permute-start.4 = (f32[1,2,8,2304]{3,2,1,0:T(8,128)S(1)}, f32[1,2,8,2304]{3,2,1,0:T(8,128)S(1)}, u32[]{:S(2)}, u32[]{:S(2)}) collective-permute-start(f32[1,2,8,2304]{3,2,1,0:T(8,128)S(1)} %get-tuple-element.24), channel_id=1, source_target_pairs={{1,0},{2,1},{3,2},{5,4},{6,5},{7,6},{9,8},{10,9},{11,10},{13,12},{... | collective-permute-start | bytes 442376 | tf_op jit(solution)/shard_map/ppermute | solution.py:24
  129.8 8.4 %collective-permute-start.5 = (f32[1,2,8,2304]{3,2,1,0:T(8,128)S(1)}, f32[1,2,8,2304]{3,2,1,0:T(8,128)S(1)}, u32[]{:S(2)}, u32[]{:S(2)}) collective-permute-start(f32[1,2,8,2304]{3,2,1,0:T(8,128)S(1)} %get-tuple-element.25), channel_id=1, source_target_pairs={{0,1},{1,2},{2,3},{4,5},{5,6},{6,7},{8,9},{9,10},{10,11},{12,13},{... | collective-permute-start | bytes 442376 | tf_op jit(solution)/shard_map/ppermute | solution.py:21
  138.2 0.6 fusion.55
  138.8 0.4 collective-permute-done.4
  139.2 2.3 %collective-permute-done.5 = f32[1,2,8,2304]{3,2,1,0:T(8,128)S(1)} collective-permute-done((f32[1,2,8,2304]{3,2,1,0:T(8,128)S(1)}, f32[1,2,8,2304]{3,2,1,0:T(8,128)S(1)}, u32[]{:S(2)}, u32[]{:S(2)}) %collective-permute-start.5) | collective-permute-done | bytes 147488 | tf_op jit(solution)/shard_map/ppermute | solution.py:21
  141.5 2.0 %fusion.16 = f32[12,2,8,2304]{3,2,1,0:T(8,128)S(1)} fusion(f32[12,2,8,2304]{3,2,1,0:T(8,128)S(1)} %fusion.22, f32[1,2,8,2304]{3,2,1,0:T(8,128)S(1)} %collective-permute-done.5, f32[1,2,8,2304]{3,2,1,0:T(8,128)S(1)} %collective-permute-done.4, f32[12,2,8,2303]{3,2,1,0:T(8,128)S(1)} %get-tuple-element.23, f32[12,2,8,2303]{3,2,1,0:T(8,128)S(1)} %get-tuple-element.22, ...), kind=kLoop, calls=%fused_computation.36 | loop fusion | flops 10616832 | bytes 13345856 | tf_op jit(solution)/shard_map/div | solution.py:159
  143.6 0.6 fusion.53
  144.2 1.9 %collective-permute-start.6 = (f32[1,2,8,2304]{3,2,1,0:T(8,128)S(1)}, f32[1,2,8,2304]{3,2,1,0:T(8,128)S(1)}, u32[]{:S(2)}, u32[]{:S(2)}) collective-permute-start(f32[1,2,8,2304]{3,2,1,0:T(8,128)S(1)} %get-tuple-element.18), channel_id=1, source_target_pairs={{1,0},{2,1},{3,2},{5,4},{6,5},{7,6},{9,8},{10,9},{11,10},{13,12},{... | collective-permute-start | bytes 442376 | tf_op jit(solution)/shard_map/ppermute | solution.py:24
  146.1 8.4 %collective-permute-start.7 = (f32[1,2,8,2304]{3,2,1,0:T(8,128)S(1)}, f32[1,2,8,2304]{3,2,1,0:T(8,128)S(1)}, u32[]{:S(2)}, u32[]{:S(2)}) collective-permute-start(f32[1,2,8,2304]{3,2,1,0:T(8,128)S(1)} %get-tuple-element.19), channel_id=1, source_target_pairs={{0,1},{1,2},{2,3},{4,5},{5,6},{6,7},{8,9},{9,10},{10,11},{12,13},{... | collective-permute-start | bytes 442376 | tf_op jit(solution)/shard_map/ppermute | solution.py:21
  154.5 0.6 fusion.52
  155.1 0.4 collective-permute-done.6
  155.5 2.3 %collective-permute-done.7 = f32[1,2,8,2304]{3,2,1,0:T(8,128)S(1)} collective-permute-done((f32[1,2,8,2304]{3,2,1,0:T(8,128)S(1)}, f32[1,2,8,2304]{3,2,1,0:T(8,128)S(1)}, u32[]{:S(2)}, u32[]{:S(2)}) %collective-permute-start.7) | collective-permute-done | bytes 147488 | tf_op jit(solution)/shard_map/ppermute | solution.py:21
  157.8 2.9 %fusion.10 = f32[12,2,8,2304]{3,2,1,0:T(8,128)} fusion(f32[12,2,8,2304]{3,2,1,0:T(8,128)S(1)} %fusion.16, f32[1,2,8,2304]{3,2,1,0:T(8,128)S(1)} %collective-permute-done.7, f32[1,2,8,2304]{3,2,1,0:T(8,128)S(1)} %collective-permute-done.6, f32[12,2,8,2303]{3,2,1,0:T(8,128)S(1)} %get-tuple-element.17, f32[12,2,8,2303]{3,2,1,0:T(8,128)S(1)} %get-tuple-element.16, ...), kind=kLoop, calls=%fused_computation.28 | loop fusion | flops 10616832 | bytes 13345856 | tf_op jit(solution)/shard_map/div | solution.py:159
  (28 shorter events, 0.2 us)
Async XLA Ops:
  0.0 107.0 %collective-permute-start = (f32[12,2,8,2304]{3,2,1,0:T(8,128)}, f32[12,2,8,2304]{3,2,1,0:T(8,128)S(1)}, u32[]{:S(2)}, u32[]{:S(2)}) collective-permute-start(f32[12,2,8,2304]{3,2,1,0:T(8,128)} %param.2), channel_id=1, source_target_pairs={{4,0},{8,4},{12,8},{16,12},{20,16},{24,20},{28,24},{32,28},{36,32}... | collective-permute-start | bytes 5308424 | tf_op jit(solution)/shard_map/ppermute | solution.py:24
  13.5 93.5 %collective-permute-start.1 = (f32[12,2,8,2304]{3,2,1,0:T(8,128)}, f32[12,2,8,2304]{3,2,1,0:T(8,128)}, u32[]{:S(2)}, u32[]{:S(2)}) collective-permute-start(f32[12,2,8,2304]{3,2,1,0:T(8,128)} %param.2), channel_id=1, source_target_pairs={{0,4},{4,8},{8,12},{12,16},{16,20},{20,24},{24,28},{28,32},{32,36}... | collective-permute-start | bytes 5308424 | tf_op jit(solution)/shard_map/ppermute | solution.py:21
  16.6 0.6 copy-start.1
  16.8 0.6 copy-start.2
  16.9 0.6 copy-start.6
  17.5 89.5 %copy-start = (f32[12,2,8,2304]{3,2,1,0:T(8,128)S(1)}, f32[12,2,8,2304]{3,2,1,0:T(8,128)}, u32[]{:S(2)}) copy-start(f32[12,2,8,2304]{3,2,1,0:T(8,128)} %param.2) | copy-start | bytes 5308420
  97.0 0.6 copy-start.11
  112.9 10.5 %collective-permute-start.2 = (f32[1,2,8,2304]{3,2,1,0:T(8,128)S(1)}, f32[1,2,8,2304]{3,2,1,0:T(8,128)S(1)}, u32[]{:S(2)}, u32[]{:S(2)}) collective-permute-start(f32[1,2,8,2304]{3,2,1,0:T(8,128)S(1)} %get-tuple-element.30), channel_id=1, source_target_pairs={{1,0},{2,1},{3,2},{5,4},{6,5},{7,6},{9,8},{10,9},{11,10},{13,12},{... | collective-permute-start | bytes 442376 | tf_op jit(solution)/shard_map/ppermute | solution.py:24
  115.0 10.0 %copy-start.3 = (f32[12,2,8]{2,1,0:T(2,128)S(1)}, f32[12,2,8]{2,1,0:T(2,128)}, u32[]{:S(2)}) copy-start(f32[12,2,8]{2,1,0:T(2,128)} %copy.11) | copy-start | bytes 2308
  115.0 10.0 %copy-start.4 = (f32[12,2,8]{2,1,0:T(2,128)S(1)}, f32[12,2,8]{2,1,0:T(2,128)}, u32[]{:S(2)}) copy-start(f32[12,2,8]{2,1,0:T(2,128)} %copy.12) | copy-start | bytes 2308
  115.1 10.0 %copy-start.5 = (f32[12,2,8]{2,1,0:T(2,128)S(1)}, f32[12,2,8]{2,1,0:T(2,128)}, u32[]{:S(2)}) copy-start(f32[12,2,8]{2,1,0:T(2,128)} %copy.10) | copy-start | bytes 2308
  115.1 10.0 %copy-start.7 = (f32[2,8]{1,0:T(2,128)S(1)}, f32[2,8]{1,0:T(2,128)}, u32[]{:S(2)}) copy-start(f32[2,8]{1,0:T(2,128)} %get-tuple-element.61) | copy-start | bytes 196
  115.1 10.0 %copy-start.8 = (f32[2,8]{1,0:T(2,128)S(1)}, f32[2,8]{1,0:T(2,128)}, u32[]{:S(2)}) copy-start(f32[2,8]{1,0:T(2,128)} %get-tuple-element.62) | copy-start | bytes 196
  115.1 10.0 %copy-start.9 = (f32[2,8]{1,0:T(2,128)S(1)}, f32[2,8]{1,0:T(2,128)}, u32[]{:S(2)}) copy-start(f32[2,8]{1,0:T(2,128)} %get-tuple-element.63) | copy-start | bytes 196
  115.1 10.0 %copy-start.10 = (f32[2,8]{1,0:T(2,128)S(1)}, f32[2,8]{1,0:T(2,128)}, u32[]{:S(2)}) copy-start(f32[2,8]{1,0:T(2,128)} %get-tuple-element.65) | copy-start | bytes 196
  115.1 10.0 %collective-permute-start.3 = (f32[1,2,8,2304]{3,2,1,0:T(8,128)S(1)}, f32[1,2,8,2304]{3,2,1,0:T(8,128)S(1)}, u32[]{:S(2)}, u32[]{:S(2)}) collective-permute-start(f32[1,2,8,2304]{3,2,1,0:T(8,128)S(1)} %get-tuple-element.31), channel_id=1, source_target_pairs={{0,1},{1,2},{2,3},{4,5},{5,6},{6,7},{8,9},{9,10},{10,11},{12,13},{... | collective-permute-start | bytes 442376 | tf_op jit(solution)/shard_map/ppermute | solution.py:21
  127.8 11.3 %collective-permute-start.4 = (f32[1,2,8,2304]{3,2,1,0:T(8,128)S(1)}, f32[1,2,8,2304]{3,2,1,0:T(8,128)S(1)}, u32[]{:S(2)}, u32[]{:S(2)}) collective-permute-start(f32[1,2,8,2304]{3,2,1,0:T(8,128)S(1)} %get-tuple-element.24), channel_id=1, source_target_pairs={{1,0},{2,1},{3,2},{5,4},{6,5},{7,6},{9,8},{10,9},{11,10},{13,12},{... | collective-permute-start | bytes 442376 | tf_op jit(solution)/shard_map/ppermute | solution.py:24
  129.8 11.7 %collective-permute-start.5 = (f32[1,2,8,2304]{3,2,1,0:T(8,128)S(1)}, f32[1,2,8,2304]{3,2,1,0:T(8,128)S(1)}, u32[]{:S(2)}, u32[]{:S(2)}) collective-permute-start(f32[1,2,8,2304]{3,2,1,0:T(8,128)S(1)} %get-tuple-element.25), channel_id=1, source_target_pairs={{0,1},{1,2},{2,3},{4,5},{5,6},{6,7},{8,9},{9,10},{10,11},{12,13},{... | collective-permute-start | bytes 442376 | tf_op jit(solution)/shard_map/ppermute | solution.py:21
  144.2 11.3 %collective-permute-start.6 = (f32[1,2,8,2304]{3,2,1,0:T(8,128)S(1)}, f32[1,2,8,2304]{3,2,1,0:T(8,128)S(1)}, u32[]{:S(2)}, u32[]{:S(2)}) collective-permute-start(f32[1,2,8,2304]{3,2,1,0:T(8,128)S(1)} %get-tuple-element.18), channel_id=1, source_target_pairs={{1,0},{2,1},{3,2},{5,4},{6,5},{7,6},{9,8},{10,9},{11,10},{13,12},{... | collective-permute-start | bytes 442376 | tf_op jit(solution)/shard_map/ppermute | solution.py:24
  146.1 11.7 %collective-permute-start.7 = (f32[1,2,8,2304]{3,2,1,0:T(8,128)S(1)}, f32[1,2,8,2304]{3,2,1,0:T(8,128)S(1)}, u32[]{:S(2)}, u32[]{:S(2)}) collective-permute-start(f32[1,2,8,2304]{3,2,1,0:T(8,128)S(1)} %get-tuple-element.19), channel_id=1, source_target_pairs={{0,1},{1,2},{2,3},{4,5},{5,6},{6,7},{8,9},{9,10},{10,11},{12,13},{... | collective-permute-start | bytes 442376 | tf_op jit(solution)/shard_map/ppermute | solution.py:21
